TPU v7x, 32 devices: a whole 2x2x4 slice. The times are simulated.
32 devices in a mesh: row: 4 (over z), col: 4 (over y, x), pair: 2 (over core).
Axes of the slice: x: 2, y: 2, z: 4, core: 2. Of those that a mesh axis runs over, the one named last changes fastest.
Arguments:
- integrals: bfloat16 [2048, 2048], P('row', ('col', 'pair')), may hold values from -0.1875 to 0.1875
- int_mask: int32 [32, 32], P('row', ('col', 'pair')), may hold values 0 or 1
- amplitudes: bfloat16 [2048, 2048], P('row', ('col', 'pair')), may hold values from -6 to 6
- domain_mask: int32 [32, 2048], P('row', ('col', 'pair')), may hold values 0 or 1
- virt_energy: float32 [2048], P('row'), may hold values from 0.5 to 4
- occ_energy: float32 [2048], P(('col', 'pair')), may hold values from -3 to -0.5
Outputs:
- update: float32 [2048, 2048], P('row', ('col', 'pair'))
All inputs are finite; a program needn't handle non-finite values. No bound on the sum of `int_mask` or of `domain_mask` on one device may be relied on, other than what follows from the above.
Results may differ from a plain program's by a relative error of at most 0.0003.
Values may be sent and summed in bfloat16 or wider, within the bound.
A program may use at most 64 MiB of HBM per device.

v0:
```python
import jax
import jax.numpy as jnp
from jax import lax
from jax.sharding import PartitionSpec as P

TILE = 64


def mask_tiles(values, tile_mask):
    shaped = values.reshape(tile_mask.shape[0], TILE, tile_mask.shape[1], TILE)
    return (shaped * tile_mask[:, None, :, None].astype(values.dtype)).reshape(values.shape)


def mask_rows(values, row_mask):
    shaped = values.reshape(row_mask.shape[0], TILE, values.shape[1])
    return (shaped * row_mask[:, None, :].astype(values.dtype)).reshape(values.shape)


def local(integrals, int_mask, amplitudes, domain_mask, virt_energy, occ_energy):
    masked_ints = mask_tiles(integrals, int_mask)
    masked_amps = mask_rows(amplitudes, domain_mask)
    amps_whole = lax.all_gather(masked_amps, "row", axis=0, tiled=True)
    ladder = jnp.dot(
        lax.all_gather(masked_ints, ("col", "pair"), axis=1, tiled=True),
        amps_whole,
        preferred_element_type=jnp.float32,
    )
    denominator = virt_energy[:, None] - occ_energy[None, :]
    scaled = ladder / denominator
    return mask_rows(scaled, domain_mask)


def solution(mesh):
    placed = (
        P("row", ("col", "pair")),
        P("row", ("col", "pair")),
        P("row", ("col", "pair")),
        P("row", ("col", "pair")),
        P("row"),
        P(("col", "pair")),
    )
    return jax.shard_map(
        local, mesh=mesh, in_specs=placed, out_specs=P("row", ("col", "pair")), check_vma=False
    )
```

profile of v0, /device:TPU:0, one launch (start us, length us, event | category | flops | bytes accessed | tf_op | source)
XLA Modules:
  0.0 79.7 jit_solution(4837821829733445716)
XLA Ops:
  6.5 0.0 copy-start
  6.5 0.0 copy-start.2
  6.5 0.0 copy-start.1
  6.5 0.0 all-gather.5.cloned.1.call-start
  6.5 0.8 fusion.1
  7.3 1.7 %bitcast_multiply_fusion = bf16[512,256]{1,0:T(8,128)(2,1)} fusion(bf16[512,256]{1,0:T(8,128)(2,1)} %param.8, bf16[8,256]{1,0:T(8,128)(2,1)S(1)} %get-tuple-element.5), kind=kLoop, calls=%fused_computation.2 | loop fusion | flops 131072 | bytes 528384 | tf_op jit(solution)/shard_map/mul | solution.py:16
  9.0 0.0 all-gather.5.cloned.1.call-update
  9.0 0.0 all-gather.3.cloned.1.call-start
  9.1 0.7 convert_element_type.12
  9.8 0.1 copy.7
  9.9 0.2 mul.33
  10.1 0.3 mul.34
  10.4 0.0 copy-done
  10.4 0.8 mul.35
  11.2 0.0 all-gather.3.cloned.1.call-update
  11.2 28.6 %all-gather.5.cloned.1.call-done = bf16[2048,256]{1,0:T(8,128)(2,1)} async-done(((bf16[512,256]{1,0:T(8,128)(2,1)}), bf16[2048,256]{1,0:T(8,128)(2,1)}) %all-gather.5.cloned.1.call-update) | async-done | bytes 1048592 | tf_op jit(solution)/shard_map/all_gather | solution.py:22
  39.8 29.6 %all-gather.3.cloned.1.call-done = bf16[512,2048]{1,0:T(8,128)(2,1)} async-done(((bf16[512,256]{1,0:T(8,128)(2,1)}), bf16[512,2048]{1,0:T(8,128)(2,1)}) %all-gather.3.cloned.1.call-update) | async-done | bytes 2097168 | tf_op jit(solution)/shard_map/all_gather | solution.py:24
  69.4 0.0 copy-done.2
  69.5 0.0 copy-done.1
  69.5 3.4 %fusion = f32[512,256]{1,0:T(8,128)} fusion(f32[512,256]{1,0:T(8,128)S(1)} %bitcast.5, bf16[512,2048]{1,0:T(8,128)(2,1)} %all-gather.3.cloned.1.call-done, bf16[2048,256]{1,0:T(8,128)(2,1)} %all-gather.5.cloned.1.call-done, f32[256]{0:T(256)S(1)} %copy-done.2, f32[512]{0:T(512)S(1)} %copy-done.1), kind=kOutput, calls=%fused_computation.1 | convolution fusion | flops 537264128 | bytes 4197376 | tf_op jit(solution)/shard_map/dot_general | solution.py:23
  (1 shorter events, 0.0 us)
Async XLA Ops:
  6.5 3.9 %copy-start = (bf16[512,256]{1,0:T(8,128)(2,1)S(1)}, bf16[512,256]{1,0:T(8,128)(2,1)}, u32[]{:S(2)}) copy-start(bf16[512,256]{1,0:T(8,128)(2,1)} %param.6) | copy-start | bytes 786436
  6.5 62.9 %copy-start.2 = (f32[256]{0:T(256)S(1)}, f32[256]{0:T(256)}, u32[]{:S(2)}) copy-start(f32[256]{0:T(256)} %param.11) | copy-start | bytes 3076
  6.5 62.9 %copy-start.1 = (f32[512]{0:T(512)S(1)}, f32[512]{0:T(512)}, u32[]{:S(2)}) copy-start(f32[512]{0:T(512)} %param.10) | copy-start | bytes 6148
  6.5 33.3 %all-gather.5.cloned.1.call-start = ((), (), s32[]{:S(2)}) async-start(), calls=%async_computation.1 | async-start | bytes 1310720 | tf_op jit(solution)/shard_map/all_gather | solution.py:22
  9.0 60.4 %all-gather.3.cloned.1.call-start = ((), (), s32[]{:S(2)}) async-start(), calls=%async_computation | async-start | bytes 2359296 | tf_op jit(solution)/shard_map/all_gather | solution.py:24
Sparse Core Ops, SparseCore 0:
  9.1 30.6 all-gather.4
  41.7 27.6 all-gather.2
where the time goes:
time: 79.9 us; the launch traced here: 79.7 us
  waiting for transfers between devices  58.2 us (73%)
  between operations  13.4 us (17%)
  other arithmetic  3.9 us (5%)
  matrix products  3.37 us (4%)
    all_gather x1, waiting for transfers between devices, local(): lax.all_gather(masked_ints, ('col', 'pair'), axis=1, tiled=True)  29.6 us
    all_gather x1, waiting for transfers between devices, local(): amps_whole = lax.all_gather(masked_amps, 'row', axis=0, tiled=True)  28.6 us
    dot_general x1, matrix products, local(): jnp.dot(lax.all_gather(masked_ints, ('col', 'pair'), axis=1, tiled=True),...  3.37 us
    mul x1, other arithmetic, mask_rows(): shaped * row_mask[:, None, :].astype(values.dtype)  1.67 us
  transfers between devices with their start and end apart: 2, of which 2 were waited for; matrix products, arithmetic and copies ran while one was open for 3% of the time, Pallas kernels for 0%

commit v1 on v0

--- a/solution.py
+++ b/solution.py
@@ -4,6 +4,20 @@
 from jax.sharding import PartitionSpec as P
 
 TILE = 64
+
+
+def spread_slots(local_values, axis_tag):
+    num_devices = lax.axis_size(axis_tag)
+    ready = local_values
+    arrivals = [ready]
+    prior = sorted(((ix, (ix + 1) % num_devices) for ix in range(num_devices)))
+    for dev_j in tuple(range(1, num_devices)):
+        ready = lax.ppermute(ready, axis_name=axis_tag, perm=prior)
+        arrivals.insert(0, ready)
+    local_next = jnp.concatenate(arrivals, 0)
+    block_next = lax.axis_index(axis_tag)
+    even = block_next + 1
+    return jnp.roll(local_next, even * local_values.shape[0], axis=0)
 
 
 def mask_tiles(values, tile_mask):
@@ -19,7 +33,7 @@
 def local(integrals, int_mask, amplitudes, domain_mask, virt_energy, occ_energy):
     masked_ints = mask_tiles(integrals, int_mask)
     masked_amps = mask_rows(amplitudes, domain_mask)
-    amps_whole = lax.all_gather(masked_amps, "row", axis=0, tiled=True)
+    amps_whole = spread_slots(masked_amps, "row")
     ladder = jnp.dot(
         lax.all_gather(masked_ints, ("col", "pair"), axis=1, tiled=True),
         amps_whole,

time: 79.9 us -> 51 us (0.64)
  waiting for transfers between devices: 58.2 us -> 27.7 us
  starting transfers between devices: 0.04 us -> 3.08 us
  other arithmetic: 3.9 us -> 2.5 us
    all_gather x1 -> x0, waiting for transfers between devices: 28.6 us -> none  [local(): amps_whole = lax.all_gather(masked_amps, 'row', axis=0, tiled=True)]
    all_gather x1, waiting for transfers between devices: 29.6 us -> 1.69 us  [local(): lax.all_gather(masked_ints, ('col', 'pair'), axis=1, tiled=True)]
    ppermute x0 -> x3, waiting for transfers between devices: none -> 26 us  [spread_slots(): ready = lax.ppermute(ready, axis_name=axis_tag, perm=prior)]
    ppermute x0 -> x3, starting transfers between devices: none -> 3.08 us  [spread_slots(): ready = lax.ppermute(ready, axis_name=axis_tag, perm=prior)]
    mul x1, other arithmetic: 1.67 us -> 0.02 us  [mask_rows(): shaped * row_mask[:, None, :].astype(values.dtype)]
    mul x1, other arithmetic: 0.77 us -> 1.74 us  [mask_tiles(): shaped * tile_mask[:, None, :, None].astype(values.dtype)]
  transfers between devices with their start and end apart: 2 -> 4, of which waited for: 2 -> 4; matrix products, arithmetic and copies ran while one was open for 3% -> 0% of each run, Pallas kernels for 0% -> 0%
where the time goes in v1:
time: 51 us; the launch traced here: 50.8 us
  waiting for transfers between devices  27.7 us (54%)
  between operations  13.5 us (26%)
  matrix products  3.13 us (6%)
  starting transfers between devices  3.08 us (6%)
  other arithmetic  2.5 us (5%)
  local copies, waits for them, and re-layouts  0.85 us (2%)
    ppermute x3, waiting for transfers between devices, spread_slots(): ready = lax.ppermute(ready, axis_name=axis_tag, perm=prior)  26 us
    dot_general x1, matrix products, local(): jnp.dot(lax.all_gather(masked_ints, ('col', 'pair'), axis=1, tiled=True),...  3.13 us
    ppermute x3, starting transfers between devices, spread_slots(): ready = lax.ppermute(ready, axis_name=axis_tag, perm=prior)  3.08 us
    mul x1, other arithmetic, mask_tiles(): shaped * tile_mask[:, None, :, None].astype(values.dtype)  1.74 us
    all_gather x1, waiting for transfers between devices, local(): lax.all_gather(masked_ints, ('col', 'pair'), axis=1, tiled=True)  1.69 us
  transfers between devices with their start and end apart: 4, of which 4 were waited for; matrix products, arithmetic and copies ran while one was open for 0% of the time, Pallas kernels for 0%

profile of v1, /device:TPU:0, one launch (start us, length us, event | category | flops | bytes accessed | tf_op | source)
XLA Modules:
  0.0 50.8 jit_solution(13573399815835494730)
XLA Ops:
  6.5 0.0 copy-start.1
  6.5 0.0 copy-start
  6.5 0.0 all-gather.2.cloned.1.call-start
  6.5 0.7 %convert_element_type.12 = bf16[8,4]{0,1:T(4,128)(2,1)S(1)} convert(s32[8,4]{0,1:T(4,128)} %param.7) | non-fusion elementwise | flops 32 | bytes 192 | tf_op jit(solution)/shard_map/convert_element_type | solution.py:25
  7.3 0.1 copy.7
  7.4 0.2 mul.36
  7.6 0.3 mul.37
  7.9 1.7 %mul.38 = bf16[512,256]{1,0:T(8,128)(2,1)} multiply(bf16[512,256]{1,0:T(8,128)(2,1)} %param.6, bf16[512,256]{1,0:T(8,128)(2,1)S(1)} %mul.37) | non-fusion elementwise | flops 131072 | bytes 786432 | tf_op jit(solution)/shard_map/mul | solution.py:25
  9.7 0.0 all-gather.2.cloned.1.call-update
  9.7 0.0 copy-done.1
  9.7 0.0 copy-done
  9.8 3.1 %collective-permute-start = (bf16[512,256]{1,0:T(8,128)(2,1)S(1)}, bf16[512,256]{1,0:T(8,128)(2,1)S(1)}, u32[]{:S(2)}, u32[]{:S(2)}) collective-permute-start(bf16[512,256]{1,0:T(8,128)(2,1)S(1)} %bitcast_multiply_fusion), channel_id=1, source_target_pairs={{0,8},{8,16},{16,24},{24,0},{1,9},{9,17},{17,25},{25,1},{2,10},{10... | collective-permute-start | bytes 786440 | tf_op jit(solution)/shard_map/ppermute | solution.py:15
  12.8 8.3 %collective-permute-done = bf16[512,256]{1,0:T(8,128)(2,1)S(1)} collective-permute-done((bf16[512,256]{1,0:T(8,128)(2,1)S(1)}, bf16[512,256]{1,0:T(8,128)(2,1)S(1)}, u32[]{:S(2)}, u32[]{:S(2)}) %collective-permute-start) | collective-permute-done | bytes 262176 | tf_op jit(solution)/shard_map/ppermute | solution.py:15
  21.2 0.0 collective-permute-start.1
  21.2 9.3 %collective-permute-done.1 = bf16[512,256]{1,0:T(8,128)(2,1)S(1)} collective-permute-done((bf16[512,256]{1,0:T(8,128)(2,1)S(1)}, bf16[512,256]{1,0:T(8,128)(2,1)S(1)}, u32[]{:S(2)}, u32[]{:S(2)}) %collective-permute-start.1) | collective-permute-done | bytes 262176 | tf_op jit(solution)/shard_map/ppermute | solution.py:15
  30.5 0.0 collective-permute-start.2
  30.5 8.4 %collective-permute-done.2 = bf16[512,256]{1,0:T(8,128)(2,1)S(1)} collective-permute-done((bf16[512,256]{1,0:T(8,128)(2,1)S(1)}, bf16[512,256]{1,0:T(8,128)(2,1)S(1)}, u32[]{:S(2)}, u32[]{:S(2)}) %collective-permute-start.2) | collective-permute-done | bytes 262176 | tf_op jit(solution)/shard_map/ppermute | solution.py:15
  38.8 0.0 copy-start.2
  38.9 0.0 copy-start.3
  39.1 1.7 %all-gather.2.cloned.1.call-done = bf16[512,2048]{1,0:T(8,128)(2,1)} async-done(((bf16[512,256]{1,0:T(8,128)(2,1)}), bf16[512,2048]{1,0:T(8,128)(2,1)}) %all-gather.2.cloned.1.call-update) | async-done | bytes 2097168 | tf_op jit(solution)/shard_map/all_gather | solution.py:38
  40.8 0.0 copy-done.2
  40.8 0.0 copy-done.3
  40.8 3.1 %fusion = f32[512,256]{1,0:T(8,128)} fusion(f32[512,256]{1,0:T(8,128)S(1)} %bitcast.4, bf16[512,2048]{1,0:T(8,128)(2,1)} %all-gather.2.cloned.1.call-done, bf16[4096,256]{1,0:T(8,128)(2,1)S(1)} %constant_dynamic-update-slice_fusion, s32[]{:T(128)S(6)} %select_n.14, f32[256]{0:T(256)S(1)} %copy-done.3, f32[512]{0:T(512)S(1)} %copy-done.2), kind=kOutput, calls=%fused_computation.1 | convolution fusion | flops 537264128 | bytes 4197380 | tf_op jit(solution)/shard_map/dot_general | solution.py:37
  (11 shorter events, 0.2 us)
Async XLA Ops:
  6.5 3.2 %copy-start.1 = (s32[8,256]{1,0:T(8,128)S(1)}, s32[8,256]{1,0:T(8,128)}, u32[]{:S(2)}) copy-start(s32[8,256]{1,0:T(8,128)} %param.9) | copy-start | bytes 24580
  6.5 3.2 %copy-start = (bf16[512,256]{1,0:T(8,128)(2,1)S(1)}, bf16[512,256]{1,0:T(8,128)(2,1)}, u32[]{:S(2)}) copy-start(bf16[512,256]{1,0:T(8,128)(2,1)} %param.8) | copy-start | bytes 786436
  6.5 34.2 %all-gather.2.cloned.1.call-start = ((), (), s32[]{:S(2)}) async-start(), calls=%async_computation | async-start | bytes 2359296 | tf_op jit(solution)/shard_map/all_gather | solution.py:38
  9.8 11.4 %collective-permute-start = (bf16[512,256]{1,0:T(8,128)(2,1)S(1)}, bf16[512,256]{1,0:T(8,128)(2,1)S(1)}, u32[]{:S(2)}, u32[]{:S(2)}) collective-permute-start(bf16[512,256]{1,0:T(8,128)(2,1)S(1)} %bitcast_multiply_fusion), channel_id=1, source_target_pairs={{0,8},{8,16},{16,24},{24,0},{1,9},{9,17},{17,25},{25,1},{2,10},{10... | collective-permute-start | bytes 786440 | tf_op jit(solution)/shard_map/ppermute | solution.py:15
  21.2 9.3 %collective-permute-start.1 = (bf16[512,256]{1,0:T(8,128)(2,1)S(1)}, bf16[512,256]{1,0:T(8,128)(2,1)S(1)}, u32[]{:S(2)}, u32[]{:S(2)}) collective-permute-start(bf16[512,256]{1,0:T(8,128)(2,1)S(1)} %collective-permute-done), channel_id=1, source_target_pairs={{0,8},{8,16},{16,24},{24,0},{1,9},{9,17},{17,25},{25,1},{2,10},{10... | collective-permute-start | bytes 786440 | tf_op jit(solution)/shard_map/ppermute | solution.py:15
  30.5 8.4 %collective-permute-start.2 = (bf16[512,256]{1,0:T(8,128)(2,1)S(1)}, bf16[512,256]{1,0:T(8,128)(2,1)S(1)}, u32[]{:S(2)}, u32[]{:S(2)}) collective-permute-start(bf16[512,256]{1,0:T(8,128)(2,1)S(1)} %collective-permute-done.1), channel_id=1, source_target_pairs={{0,8},{8,16},{16,24},{24,0},{1,9},{9,17},{17,25},{25,1},{2,10},{10... | collective-permute-start | bytes 786440 | tf_op jit(solution)/shard_map/ppermute | solution.py:15
  38.8 1.9 %copy-start.2 = (f32[512]{0:T(512)S(1)}, f32[512]{0:T(512)}, u32[]{:S(2)}) copy-start(f32[512]{0:T(512)} %param.10) | copy-start | bytes 6148
  38.9 1.9 %copy-start.3 = (f32[256]{0:T(256)S(1)}, f32[256]{0:T(256)}, u32[]{:S(2)}) copy-start(f32[256]{0:T(256)} %param.11) | copy-start | bytes 3076
Sparse Core Ops, SparseCore 0:
  9.8 30.8 all-gather.1
